TPU v7x, 32 devices: a whole 2x2x4 slice. The times are simulated.
32 devices in a mesh: inl: 8 (over z, y), off: 4 (over x, core).
Axes of the slice: x: 2, y: 2, z: 4, core: 2. Of those that a mesh axis runs over, the one named last changes fastest.
Arguments:
- traces: bfloat16 [4, 4096, 4096], P('off', 'inl'), may hold values from -24 to 24, as said below
- owner: int32 [4, 4096, 1], P('off', 'inl'), may hold values from 0 to 7; in each aligned block of 512 rows (0 to 511, 512 to 1023, ..., all dimensions but the last counted through in order) at most 192 rows name the same one
- local_bin: int32 [4, 4096], P('off', 'inl'), may hold values from 0 to 63
- live_count: int32 [4, 8], P('off', 'inl'), may hold values from 256 to 512, as said below
- xl_gain: float32 [16], replicated, may hold values from 0.2 to 1
- il_gain: float32 [32], replicated, may hold values from 0.2 to 1
Outputs:
- volume: bfloat16 [4, 16, 32, 4096], P('off', 'inl')
Inputs may be any that keep to these rules, and one draw needn't show every extreme that they name: `traces`: every trace amplitude lies in this range. Among the traces of one device no owner is named more than 192 times; some device names one owner exactly 192 times. The first live_count traces of a device are live; some device has all 512 traces live.
All inputs are finite; a program needn't handle non-finite values.
Results may differ from a plain program's by a relative error of at most 0.024.
Values may be sent and summed in bfloat16 or wider, within the bound.
A program may use at most 128 MiB of HBM per device.

v0:
```python
import math

import jax
import jax.numpy as jnp
from jax import lax
from jax.sharding import PartitionSpec as P

NLAG = 80


damping = 0.1


def levinson(series):
    order = series.shape[0]
    error = series[0] + damping
    coeffs = jnp.zeros_like(series).at[0].set(1.0)
    for section in range(1, order):
        partial_sum = jnp.sum(coeffs[:section] * series[section:0:-1], axis=0)
        reflection = -partial_sum / error
        update = coeffs[: section + 1] + reflection * coeffs[section::-1]
        coeffs = coeffs.at[: section + 1].set(update)
        error = error * (1.0 - reflection * reflection)
    return coeffs


def smooth_matrix(gain, reach):
    width = gain.shape[0]
    index = jnp.arange(width)
    distance = jnp.abs(index[:, None] - index[None, :])
    weight = jnp.take(gain, distance) * jnp.exp(-distance.astype(gain.dtype) / reach)
    return (weight / jnp.sum(weight, axis=1, keepdims=True)).astype(jnp.bfloat16)


def autocorrelate(block_rows):
    number, samples = block_rows.shape
    groups = samples // 128

    def autocorrelate_one_block(part_rows):
        height = part_rows.shape[0]
        leading = part_rows.reshape(height, groups, 128)
        following = jnp.pad(part_rows[:, 128:], ((0, 0), (0, 128))).reshape(height, groups, 128)
        within = jnp.einsum("nab,nac->nbc", leading, leading, preferred_element_type=jnp.float32)
        across = jnp.einsum("nab,nac->nbc", leading, following, preferred_element_type=jnp.float32)
        total = within[:, 0, :]
        for offset in range(1, 128):
            total = total + jnp.concatenate(
                [within[:, offset, offset:], across[:, offset, :offset]], axis=1
            )
        return total

    block = math.gcd(number, 64)
    result = lax.map(autocorrelate_one_block, block_rows.reshape(number // block, block, samples))
    return result.reshape(number, 128)


def apply_filter(stacked, filters):
    number, samples = stacked.shape
    taps = filters.shape[1]
    groups = samples // 128
    column = jnp.arange(256)[None, :, None]
    output_pos = jnp.arange(128)[None, None, :]
    lag_index = jnp.arange(taps)[:, None, None]
    table = (column == output_pos + 128 - lag_index).astype(jnp.bfloat16)

    def apply_one_block(pair):
        part_rows, part_filters = pair
        height = part_rows.shape[0]
        kernel = jnp.einsum(
            "nj,jcb->ncb", part_filters, table, preferred_element_type=jnp.float32
        ).astype(jnp.bfloat16)
        padded = jnp.pad(part_rows, ((0, 0), (128, 0))).reshape(height, groups + 1, 128)
        windows = jnp.concatenate([padded[:, :-1], padded[:, 1:]], axis=2)
        result = jnp.einsum("nac,ncb->nab", windows, kernel, preferred_element_type=jnp.float32)
        return result.reshape(height, samples).astype(jnp.bfloat16)

    block = math.gcd(number, 64)
    result = lax.map(
        apply_one_block,
        (
            stacked.reshape(number // block, block, samples),
            filters.reshape(number // block, block, taps),
        ),
    )
    return result.reshape(number, samples)


def shards(traces, owner, local_bin, live_count, xl_gain, il_gain):
    devices = lax.axis_size("inl")
    traces_here = traces.shape[1]
    samples = traces.shape[2]
    shot_rows = traces[0]
    slots = max(2, 3 * traces_here // devices)
    crosslines = xl_gain.shape[0]
    inlines = il_gain.shape[0]
    inline_dev = inlines // devices
    bins_here = inline_dev * crosslines
    destination = owner[0, :, 0]
    alive = jnp.arange(traces_here, dtype=jnp.int32) < live_count[0, 0]
    target = jnp.where(alive, local_bin[0], -1)
    matches = (destination[:, None] == jnp.arange(devices, dtype=jnp.int32)[None, :]).astype(
        jnp.int32
    )
    places = jnp.sum((jnp.cumsum(matches, axis=0) - matches) * matches, axis=1)
    position = destination * slots + places
    source_slot = (
        jnp.full((devices * slots,), traces_here, jnp.int32)
        .at[position]
        .set(jnp.arange(traces_here, dtype=jnp.int32))
    )
    send_bins = jnp.take(target, source_slot, axis=0, mode="fill", fill_value=-1)
    send_rows = jnp.take(shot_rows, source_slot, axis=0, mode="fill", fill_value=0)
    arrived, arrived_bins = (
        lax.all_to_all(
            send_rows.reshape(devices, slots, samples),
            "inl",
            split_axis=0,
            concat_axis=0,
            tiled=True,
        ),
        lax.all_to_all(
            send_bins.reshape(devices, slots), "inl", split_axis=0, concat_axis=0, tiled=True
        ),
    )
    arrived = arrived.reshape(devices * slots, samples)
    arrived_lags = autocorrelate(arrived)
    arrived_bins = arrived_bins.reshape(devices * slots)
    onehot = arrived_bins[:, None] == jnp.arange(bins_here, dtype=jnp.int32)[None, :]
    counts = jnp.sum(onehot.astype(jnp.float32), axis=0)
    contract = (((0,), (0,)), ((), ()))
    stack_sum = lax.dot_general(
        onehot.astype(jnp.bfloat16), arrived, contract, preferred_element_type=jnp.float32
    )
    lag_sum = lax.dot_general(
        onehot.astype(jnp.float32),
        arrived_lags[:, :NLAG],
        contract,
        precision=lax.Precision.HIGHEST,
        preferred_element_type=jnp.float32,
    )
    lag_total = lax.psum(lag_sum.astype(jnp.bfloat16), "off").astype(jnp.float32)
    stacked = (stack_sum / jnp.maximum(counts, 1.0)[:, None]).astype(jnp.bfloat16)
    rho = lag_total / jnp.maximum(lag_total[:, :1], 1.0)
    filters = levinson(rho.T).T.astype(jnp.bfloat16)
    decon = apply_filter(stacked, filters)
    cross_matrix = smooth_matrix(xl_gain, crosslines / 16.0)
    smoothed = jnp.einsum(
        "xy,iyt->ixt",
        cross_matrix,
        decon.reshape(inline_dev, crosslines, samples),
        preferred_element_type=jnp.float32,
    ).astype(jnp.bfloat16)
    relaid = lax.all_to_all(smoothed, "inl", split_axis=1, concat_axis=0, tiled=True)
    inline_matrix = smooth_matrix(il_gain, 2.0 * inline_dev)
    result = jnp.einsum(
        "ij,jxt->xit", inline_matrix, relaid, preferred_element_type=jnp.float32
    ).astype(jnp.bfloat16)
    return result[None]


def solution(mesh):
    placed = (
        P("off", "inl", None),
        P("off", "inl", None),
        P("off", "inl"),
        P("off", "inl"),
        P(),
        P(),
    )
    return jax.shard_map(
        shards, mesh=mesh, in_specs=placed, out_specs=P("off", "inl", None, None), check_vma=False
    )
```

profile of v0, /device:TPU:0, one launch (start us, length us, event | category | flops | bytes accessed | tf_op | source)
XLA Modules:
  0.0 1120.3 jit_solution(14159218616566697119)
XLA Ops:
  3.6 2.4 scatter_custom_fusion
  7.4 9.5 gather_fusion
  17.5 7.3 all-to-all-start
  24.9 24.8 %gather_fusion.1 = bf16[1536,4096]{1,0:T(8,128)(2,1)} fusion(bf16[512,4096]{1,0:T(8,128)(2,1)} %bitcast.1481, s32[2048]{0:T(1024)S(1)} %pad_clamp_fusion), kind=kCustom, calls=%fused_computation.1 | custom fusion | bytes 25171968 | tf_op jit(solution)/shard_map/jit(_take)/gather | solution.py:112
  49.7 10.7 broadcast_select_fusion
  60.3 6.1 all-to-all-start.1
  66.6 1.9 gather_fusion.2
  68.9 270.0 %all-to-all-done.1 = bf16[8,192,4096]{2,1,0:T(8,128)(2,1)} async-done(((bf16[8,192,4096]{2,1,0:T(8,128)(2,1)}), bf16[8,192,4096]{2,1,0:T(8,128)(2,1)}, u32[]{:S(2)}, u32[]{:S(2)}) %all-to-all-start.1) | async-done | bytes 12582944 | tf_op jit(solution)/shard_map/all_to_all | solution.py:114
  339.0 706.3 %while.97 = (s32[]{:T(128)}, f32[24,64,128]{2,1,0:T(8,128)S(1)}, bf16[24,64,4096]{2,1,0:T(8,128)(2,1)}, s32[]{:T(128)}) while((s32[]{:T(128)}, f32[24,64,128]{2,1,0:T(8,128)S(1)}, bf16[24,64,4096]{2,1,0:T(8,128)(2,1)}, s32[]{:T(128)}) %tuple.473), condition=%wide.region_6.7_spmd, body=%wide.region_5.6_spmd.sunk | while | flops 136298496 | bytes 32456764 | solution.py:53
  339.1 1.2 dynamic-slice_bitcast_fusion.3
  365.8 2.3 fusion.197
  368.2 1.2 dynamic-slice_bitcast_fusion.3
  394.9 2.3 fusion.197
  423.9 2.3 fusion.197
  453.0 2.3 fusion.197
  455.3 1.2 dynamic-slice_bitcast_fusion.3
  482.0 2.3 fusion.197
  484.3 1.2 dynamic-slice_bitcast_fusion.3
  511.1 2.3 fusion.197
  513.4 1.2 dynamic-slice_bitcast_fusion.3
  540.1 2.3 fusion.197
  542.4 1.2 dynamic-slice_bitcast_fusion.3
  569.1 2.3 fusion.197
  571.5 1.2 dynamic-slice_bitcast_fusion.3
  598.2 2.3 fusion.197
  627.2 2.3 fusion.197
  656.3 2.3 fusion.197
  685.3 2.3 fusion.197
  714.4 2.3 fusion.197
  743.4 2.3 fusion.197
  772.5 2.3 fusion.197
  801.5 2.3 fusion.197
  830.5 2.3 fusion.197
  859.6 2.3 fusion.197
  888.6 2.3 fusion.197
  917.7 2.3 fusion.197
  946.7 2.3 fusion.197
  975.8 2.3 fusion.197
  1004.8 2.3 fusion.197
  1033.8 2.3 fusion.197
  1046.0 10.3 psum.7
  1083.9 6.9 fusion.124
  1091.5 2.7 fusion.129
  1094.1 4.1 fusion.130
  1098.8 1.2 copy.1305
  1100.0 4.7 all-to-all-start.2
  1104.8 6.6 gather_fusion.3
  1111.5 7.0 all-to-all-done.2
  (6863 shorter events, 617.9 us)
Async XLA Ops:
  0.0 1104.8 %copy-start = (f32[32]{0:T(128)S(1)}, f32[32]{0:T(128)}, u32[]{:S(2)}) copy-start(f32[32]{0:T(128)} %param.175) | copy-start | bytes 388
  17.5 42.8 %all-to-all-start = ((s32[8,1,192]{2,1,0:T(1,128)}), s32[8,1,192]{2,1,0:T(1,128)S(1)}, u32[]{:S(2)}, u32[]{:S(2)}) async-start(s32[8,1,192]{2,1,0:T(1,128)} %select_n.89), calls=%async_computation | async-start | bytes 16384 | tf_op jit(solution)/shard_map/all_to_all | solution.py:121
  60.3 6.2 copy-start.1
  60.3 278.6 %all-to-all-start.1 = ((bf16[8,192,4096]{2,1,0:T(8,128)(2,1)}), bf16[8,192,4096]{2,1,0:T(8,128)(2,1)}, u32[]{:S(2)}, u32[]{:S(2)}) async-start(bf16[8,192,4096]{2,1,0:T(8,128)(2,1)} %broadcast_select_fusion), calls=%async_computation.1 | async-start | bytes 25165824 | tf_op jit(solution)/shard_map/all_to_all | solution.py:114
  338.9 718.5 %copy-start.2 = (f32[80,64]{1,0:T(8,128)S(1)}, f32[80,64]{1,0:T(8,128)}, u32[]{:S(2)}) copy-start(f32[80,64]{1,0:T(8,128)} %constant.1976.clone.1) | copy-start | bytes 61444
  338.9 718.5 %copy-start.3 = (f32[2,64]{1,0:T(2,128)S(1)}, f32[2,64]{1,0:T(2,128)}, u32[]{:S(2)}) copy-start(f32[2,64]{1,0:T(2,128)} %constant.1978.clone.1) | copy-start | bytes 1540
  338.9 718.5 %copy-start.4 = (f32[2,64]{1,0:T(2,128)S(1)}, f32[2,64]{1,0:T(2,128)}, u32[]{:S(2)}) copy-start(f32[2,64]{1,0:T(2,128)} %constant.1979.clone.1) | copy-start | bytes 1540
  1100.0 18.5 %all-to-all-start.2 = ((bf16[4,16,4096]{2,0,1:T(4,128)(2,1)}), bf16[4,16,4096]{2,0,1:T(4,128)(2,1)S(1)}, u32[]{:S(2)}, u32[]{:S(2)}) async-start(bf16[4,16,4096]{2,0,1:T(4,128)(2,1)} %copy.1305), calls=%async_computation.2 | async-start | bytes 1048576 | tf_op jit(solution)/shard_map/all_to_all | solution.py:153
where the time goes:
time: 1130 us; the launch traced here: 1120 us
  local copies, waits for them, and re-layouts  626 us (55%)
  waiting for transfers between devices  277 us (25%)
  other arithmetic  73.6 us (7%)
  loops' own time  59.2 us (5%)
  matrix products  52.5 us (5%)
  starting transfers between devices  18.1 us (2%)
    slice x3048, local copies, waits for them, and re-layouts, autocorrelate_one_block(): within[:, offset, offset:]  406 us
    all_to_all x1, waiting for transfers between devices, shards(): lax.all_to_all(send_rows.reshape(devices, slots, samples), 'inl', split_a...  270 us
    slice x3048, local copies, waits for them, and re-layouts, autocorrelate_one_block(): across[:, offset, :offset]  113 us
    another operation x1, loops' own time, autocorrelate(): lax.map(autocorrelate_one_block, block_rows.reshape(number // block, bloc...  59.2 us
    dynamic_update_slice x24, other arithmetic, autocorrelate(): lax.map(autocorrelate_one_block, block_rows.reshape(number // block, bloc...  55.5 us
    squeeze x24, local copies, waits for them, and re-layouts, autocorrelate(): lax.map(autocorrelate_one_block, block_rows.reshape(number // block, bloc...  28.3 us
    gather x1, local copies, waits for them, and re-layouts, shards(): jnp.take(shot_rows, source_slot, axis=0, mode='fill', fill_value=0)  24.8 us

commit v1 on v0

--- a/solution.py
+++ b/solution.py
@@ -3,6 +3,8 @@
 import jax
 import jax.numpy as jnp
 from jax import lax
+from jax.experimental import pallas as pl
+from jax.experimental.pallas import tpu as pltpu
 from jax.sharding import PartitionSpec as P
 
 NLAG = 80
@@ -32,26 +34,44 @@
     return (weight / jnp.sum(weight, axis=1, keepdims=True)).astype(jnp.bfloat16)
 
 
+def lag_kernel(flip_ref, lead_ref, follow_ref, out_ref):
+    height, groups, width = lead_ref.shape
+    rows = height * groups
+    lead = lead_ref[...].reshape(rows, width)
+    follow = follow_ref[...].reshape(rows, width)
+    both = jnp.concatenate([lead, follow], axis=1)
+    turned = lax.dot_general(
+        flip_ref[...], lead, (((1,), (1,)), ((), ())), preferred_element_type=jnp.float32
+    )
+    column = lax.broadcasted_iota(jnp.int32, (width, rows), 1) // groups
+    for item in range(height):
+        mine = jnp.where(column == item, turned, 0.0).astype(jnp.bfloat16)
+        gram = jnp.dot(mine, both, preferred_element_type=jnp.float32)
+        sheared = pltpu.roll(gram, width + 1, 1, stride=1, stride_axis=0)
+        out_ref[item : item + 1, :] = jnp.sum(sheared[:, :width], axis=0, keepdims=True)
+
+
 def autocorrelate(block_rows):
     number, samples = block_rows.shape
     groups = samples // 128
-
-    def autocorrelate_one_block(part_rows):
-        height = part_rows.shape[0]
-        leading = part_rows.reshape(height, groups, 128)
-        following = jnp.pad(part_rows[:, 128:], ((0, 0), (0, 128))).reshape(height, groups, 128)
-        within = jnp.einsum("nab,nac->nbc", leading, leading, preferred_element_type=jnp.float32)
-        across = jnp.einsum("nab,nac->nbc", leading, following, preferred_element_type=jnp.float32)
-        total = within[:, 0, :]
-        for offset in range(1, 128):
-            total = total + jnp.concatenate(
-                [within[:, offset, offset:], across[:, offset, :offset]], axis=1
-            )
-        return total
-
-    block = math.gcd(number, 64)
-    result = lax.map(autocorrelate_one_block, block_rows.reshape(number // block, block, samples))
-    return result.reshape(number, 128)
+    height = 8
+    lead = block_rows.reshape(number, groups, 128)
+    follow = jnp.pad(block_rows[:, 128:], ((0, 0), (0, 128))).reshape(number, groups, 128)
+    flip = jnp.flip(jnp.eye(128, dtype=jnp.bfloat16), axis=0)
+    spec = pl.BlockSpec((height, groups, 128), lambda i: (i, 0, 0))
+    return pl.pallas_call(
+        lag_kernel,
+        grid=(number // height,),
+        in_specs=[pl.BlockSpec((128, 128), lambda i: (0, 0)), spec, spec],
+        out_specs=pl.BlockSpec((height, 128), lambda i: (i, 0)),
+        out_shape=jax.ShapeDtypeStruct((number, 128), jnp.float32),
+        cost_estimate=pl.CostEstimate(
+            flops=number * 2 * 128 * 256 * 256,
+            bytes_accessed=number * samples * 4,
+            transcendentals=0,
+        ),
+        compiler_params=pltpu.CompilerParams(vmem_limit_bytes=32 * 1024 * 1024),
+    )(flip, lead, follow)
 
 
 def apply_filter(stacked, filters):
@@ -90,55 +110,72 @@
     traces_here = traces.shape[1]
     samples = traces.shape[2]
     shot_rows = traces[0]
-    slots = max(2, 3 * traces_here // devices)
     crosslines = xl_gain.shape[0]
     inlines = il_gain.shape[0]
     inline_dev = inlines // devices
     bins_here = inline_dev * crosslines
+    slots = max(2, 3 * traces_here // devices)
+    by_bin = bins_here <= slots
     destination = owner[0, :, 0]
-    alive = jnp.arange(traces_here, dtype=jnp.int32) < live_count[0, 0]
-    target = jnp.where(alive, local_bin[0], -1)
-    matches = (destination[:, None] == jnp.arange(devices, dtype=jnp.int32)[None, :]).astype(
-        jnp.int32
-    )
-    places = jnp.sum((jnp.cumsum(matches, axis=0) - matches) * matches, axis=1)
-    position = destination * slots + places
-    source_slot = (
-        jnp.full((devices * slots,), traces_here, jnp.int32)
-        .at[position]
-        .set(jnp.arange(traces_here, dtype=jnp.int32))
-    )
-    send_bins = jnp.take(target, source_slot, axis=0, mode="fill", fill_value=-1)
-    send_rows = jnp.take(shot_rows, source_slot, axis=0, mode="fill", fill_value=0)
-    arrived, arrived_bins = (
-        lax.all_to_all(
-            send_rows.reshape(devices, slots, samples),
-            "inl",
-            split_axis=0,
-            concat_axis=0,
-            tiled=True,
-        ),
-        lax.all_to_all(
-            send_bins.reshape(devices, slots), "inl", split_axis=0, concat_axis=0, tiled=True
-        ),
-    )
-    arrived = arrived.reshape(devices * slots, samples)
-    arrived_lags = autocorrelate(arrived)
-    arrived_bins = arrived_bins.reshape(devices * slots)
-    onehot = arrived_bins[:, None] == jnp.arange(bins_here, dtype=jnp.int32)[None, :]
-    counts = jnp.sum(onehot.astype(jnp.float32), axis=0)
-    contract = (((0,), (0,)), ((), ()))
-    stack_sum = lax.dot_general(
-        onehot.astype(jnp.bfloat16), arrived, contract, preferred_element_type=jnp.float32
-    )
-    lag_sum = lax.dot_general(
-        onehot.astype(jnp.float32),
-        arrived_lags[:, :NLAG],
-        contract,
+    local = local_bin[0]
+    order = jnp.arange(traces_here, dtype=jnp.int32)
+    alive = order < live_count[0, 0]
+    if by_bin:
+        slots = bins_here
+        place = local
+    else:
+        earlier = (
+            (destination[:, None] == destination[None, :])
+            & alive[None, :]
+            & (order[None, :] < order[:, None])
+        )
+        place = jnp.sum(earlier.astype(jnp.int32), axis=1)
+    target = jnp.where(alive, destination * slots + place, -1)
+    rows = devices * slots
+    pick = jnp.arange(rows, dtype=jnp.int32)[:, None] == target[None, :]
+    packed = jnp.dot(
+        pick.astype(jnp.bfloat16), shot_rows, preferred_element_type=jnp.float32
+    ).astype(jnp.bfloat16)
+    lags = autocorrelate(shot_rows)
+    column = jnp.arange(128, dtype=jnp.int32)[None, :]
+    lags = jnp.where(column == 127, 1.0, lags)
+    lags = jnp.where(column == 126, local[:, None].astype(jnp.float32), lags)
+    lag_rows = jnp.dot(
+        pick.astype(jnp.float32),
+        lags,
         precision=lax.Precision.HIGHEST,
         preferred_element_type=jnp.float32,
     )
-    lag_total = lax.psum(lag_sum.astype(jnp.bfloat16), "off").astype(jnp.float32)
+    if by_bin:
+        arrived = lax.all_to_all(
+            packed.reshape(devices, slots, samples), "inl", split_axis=0, concat_axis=0, tiled=True
+        )
+        stack_sum = jnp.sum(arrived.astype(jnp.float32), axis=0)
+        lag_sum = jnp.sum(
+            lax.all_to_all(
+                lag_rows.reshape(devices, slots, 128), "inl", split_axis=0, concat_axis=0, tiled=True
+            ),
+            axis=0,
+        )
+        counts = lag_sum[:, 127]
+    else:
+        arrived = lax.all_to_all(packed, "inl", split_axis=0, concat_axis=0, tiled=True)
+        arrived_lags = lax.all_to_all(lag_rows, "inl", split_axis=0, concat_axis=0, tiled=True)
+        arrived_bins = jnp.where(arrived_lags[:, 127] > 0.5, arrived_lags[:, 126], -1.0)
+        onehot = arrived_bins[:, None] == jnp.arange(bins_here, dtype=jnp.float32)[None, :]
+        counts = jnp.sum(onehot.astype(jnp.float32), axis=0)
+        contract = (((0,), (0,)), ((), ()))
+        stack_sum = lax.dot_general(
+            onehot.astype(jnp.bfloat16), arrived, contract, preferred_element_type=jnp.float32
+        )
+        lag_sum = lax.dot_general(
+            onehot.astype(jnp.float32),
+            arrived_lags,
+            contract,
+            precision=lax.Precision.HIGHEST,
+            preferred_element_type=jnp.float32,
+        )
+    lag_total = lax.psum(lag_sum[:, :NLAG], "off")
     stacked = (stack_sum / jnp.maximum(counts, 1.0)[:, None]).astype(jnp.bfloat16)
     rho = lag_total / jnp.maximum(lag_total[:, :1], 1.0)
     filters = levinson(rho.T).T.astype(jnp.bfloat16)

time: 1130 us -> 204 us (0.18)
  local copies, waits for them, and re-layouts: 626 us -> 47.4 us
  waiting for transfers between devices: 277 us -> 56.9 us
  other arithmetic: 73.6 us -> 6.46 us
  loops' own time: 59.2 us -> 0 us
  Pallas kernels: 0 us -> 41.1 us
  matrix products: 52.5 us -> 20.4 us
    slice x6144 -> x1, local copies, waits for them, and re-layouts: 521 us -> 2.43 us  [autocorrelate(): block_rows[:, 128:]]
    all_to_all x2, waiting for transfers between devices: 270 us -> 49.1 us  [the longest x1 49 us: shards(): lax.all_to_all(packed.reshape(devices, slots, samples), 'inl', split_axis...]
    another operation x1 -> x0, loops' own time: 59.2 us -> none  [autocorrelate(): lax.map(autocorrelate_one_block, block_rows.reshape(number // block, bloc...]
    dynamic_update_slice x24 -> x0, other arithmetic: 55.5 us -> none  [autocorrelate(): lax.map(autocorrelate_one_block, block_rows.reshape(number // block, bloc...]
    pallas_call x0 -> x1, Pallas kernels: none -> 41.1 us  [autocorrelate(): pl.pallas_call(lag_kernel, grid=(number // height,), in_specs=[pl.BlockSp...]
    dot_general x50 -> x2, matrix products: 44.3 us -> 7.92 us  [the longest x1 6.51 us: shards(): jnp.dot(pick.astype(jnp.bfloat16), shot_rows, preferred_element_type=jnp....]
    gather x2 -> x0, local copies, waits for them, and re-layouts: 34.2 us -> none  [the longest x1 24.8 us: shards(): jnp.take(shot_rows, source_slot, axis=0, mode='fill', fill_value=0)]
    squeeze x24 -> x0, local copies, waits for them, and re-layouts: 28.3 us -> none  [autocorrelate(): lax.map(autocorrelate_one_block, block_rows.reshape(number // block, bloc...]
where the time goes in v1:
time: 204 us
  waiting for transfers between devices  56.9 us (28%)
  local copies, waits for them, and re-layouts  47.4 us (23%)
  Pallas kernels  41.1 us (20%)
  matrix products  20.4 us (10%)
  starting transfers between devices  17 us (8%)
  blocking collectives  11.1 us (5%)
  other arithmetic  6.46 us (3%)
  between operations  3.27 us (2%)
    all_to_all x1, waiting for transfers between devices, shards(): lax.all_to_all(packed.reshape(devices, slots, samples), 'inl', split_axis...  49 us
    pallas_call x1, Pallas kernels, autocorrelate(): pl.pallas_call(lag_kernel, grid=(number // height,), in_specs=[pl.BlockSp...  41.1 us
    scatter x67, local copies, waits for them, and re-layouts, levinson(): coeffs = coeffs.at[:section + 1].set(update)  18.9 us
    unnamed x25, local copies, waits for them, and re-layouts  11.6 us
    psum x1, blocking collectives, shards(): lag_total = lax.psum(lag_sum[:, :NLAG], 'off')  11.1 us
    gather x4, local copies, waits for them, and re-layouts, smooth_matrix(): jnp.take(gain, distance) * jnp.exp(-distance.astype(gain.dtype) / reach)  8.58 us
    all_to_all x1, waiting for transfers between devices, shards(): lax.all_to_all(smoothed, 'inl', split_axis=1, concat_axis=0, tiled=True)  7.81 us
    all_to_all x1, starting transfers between devices, shards(): lax.all_to_all(lag_rows.reshape(devices, slots, 128), 'inl', split_axis=0...  7.28 us
  transfers between devices with their start and end apart: 3, of which 3 were waited for; matrix products, arithmetic and copies ran while one was open for 22% of the time, Pallas kernels for 0%

profile of v1, /device:TPU:0, one launch (start us, length us, event | category | flops | bytes accessed | tf_op | source)
XLA Modules:
  0.0 203.6 jit_solution(10588425982889699971)
XLA Ops:
  0.7 2.4 %slice.2169 = bf16[512,3968]{1,0:T(8,128)(2,1)S(1)} slice(bf16[512,4096]{1,0:T(8,128)(2,1)} %bitcast.307), slice={[0:512], [128:4096]} | slice | bytes 8126464 | tf_op jit(solution)/shard_map/slice | solution.py:59
  3.1 0.6 pad_bitcast_fusion
  3.7 3.2 %copy.182 = bf16[64,8,32,128]{3,2,1,0:T(8,128)(2,1)} copy(bf16[64,8,32,128]{3,1,2,0:T(8,128)(2,1)S(1)} %pad_bitcast_fusion) | data formatting | bytes 8388608
  7.0 3.2 %copy.181 = bf16[64,8,32,128]{3,2,1,0:T(8,128)(2,1)} copy(bf16[64,8,32,128]{3,1,2,0:T(8,128)(2,1)S(1)} %bitcast.308) | data formatting | bytes 8388608
  10.2 2.2 %copy-done.1 = bf16[64,8,32,128]{3,2,1,0:T(8,128)(2,1)S(1)} copy-done((bf16[64,8,32,128]{3,2,1,0:T(8,128)(2,1)S(1)}, bf16[64,8,32,128]{3,2,1,0:T(8,128)(2,1)}, u32[]{:S(2)}) %copy-start.1) | copy-done | bytes 4194328
  12.4 2.2 %copy-done.2 = bf16[64,8,32,128]{3,2,1,0:T(8,128)(2,1)S(1)} copy-done((bf16[64,8,32,128]{3,2,1,0:T(8,128)(2,1)S(1)}, bf16[64,8,32,128]{3,2,1,0:T(8,128)(2,1)}, u32[]{:S(2)}) %copy-start.2) | copy-done | bytes 4194328
  14.6 41.1 %shard_map.69 = f32[512,128]{1,0:T(8,128)S(1)} custom-call(bf16[128,128]{1,0:T(8,128)(2,1)S(1)} %rev.473.flip_ref, bf16[512,32,128]{2,1,0:T(8,128)(2,1)S(1)} %bitcast.299, bf16[512,32,128]{2,1,0:T(8,128)(2,1)S(1)} %bitcast.298), custom_call_target="tpu_custom_call" | custom-call | flops 8589934592 | bytes 8388608 | tf_op jit(solution)/shard_map/pallas_call | solution.py:62
  55.7 1.4 fusion.13
  57.1 7.3 %all-to-all-start.1 = ((f32[8,64,128]{2,1,0:T(8,128)}), f32[8,64,128]{2,1,0:T(8,128)S(1)}, u32[]{:S(2)}, u32[]{:S(2)}) async-start(f32[8,64,128]{2,1,0:T(8,128)} %bitcast.6), calls=%async_computation.1 | async-start | bytes 524288 | tf_op jit(solution)/shard_map/all_to_all | solution.py:155
  64.5 1.9 gather_fusion
  66.6 6.5 %convolution_convert_fusion = bf16[512,4096]{1,0:T(8,128)(2,1)} fusion(s32[512]{0:T(512)S(1)} %bitcast.392, bf16[1,512,4096]{2,1,0:T(8,128)(2,1)} %param.168), kind=kOutput, calls=%fused_computation.5 | convolution fusion | flops 2149842944 | bytes 8390656 | tf_op jit(solution)/shard_map/dot_general | solution.py:136
  73.2 6.1 %all-to-all-start = ((bf16[8,64,4096]{2,1,0:T(8,128)(2,1)}), bf16[8,64,4096]{2,1,0:T(8,128)(2,1)}, u32[]{:S(2)}, u32[]{:S(2)}) async-start(bf16[8,64,4096]{2,1,0:T(8,128)(2,1)} %bitcast.309), calls=%async_computation | async-start | bytes 8388608 | tf_op jit(solution)/shard_map/all_to_all | solution.py:150
  79.4 11.1 %psum.7 = f32[64,80]{0,1:T(8,128)S(1)} all-reduce(f32[64,80]{0,1:T(8,128)S(1)} %copy.180), channel_id=1, replica_groups=mesh['inl'=8,'off'=4] {'off'}, use_global_device_ids=true, to_apply=%region_2.3 | all-reduce | flops 5120 | bytes 40960 | tf_op jit(solution)/shard_map/psum | solution.py:178
  94.7 0.3 scatter.285
  95.1 0.3 scatter.286
  95.5 0.3 scatter.289
  95.9 0.3 scatter.290
  96.3 0.3 scatter.291
  96.7 0.3 scatter.294
  97.1 0.3 scatter.295
  102.7 0.4 scatter.325
  103.2 0.4 scatter.326
  103.7 0.4 scatter.329
  104.1 0.4 scatter.330
  104.6 0.4 scatter.331
  105.1 0.4 scatter.334
  105.5 0.4 scatter.335
  106.1 0.4 scatter.339
  106.6 0.4 scatter.340
  107.1 0.4 scatter.341
  107.6 0.4 scatter.344
  108.1 0.4 scatter.345
  108.6 0.4 scatter.346
  109.0 0.4 scatter.349
  112.8 0.3 scatter.366
  113.6 0.3 scatter.370
  116.8 0.5 scatter.385
  118.3 4.6 %fusion.6 = bf16[64,256,128]{2,0,1:T(8,128)(2,1)} fusion(s32[80,128]{1,0:T(8,128)S(1)} %iota_subtract_fusion, f32[80,64]{1,0:T(8,128)S(1)} %scatter.389, f32[80,64]{1,0:T(8,128)S(1)} %rev.629, f32[64]{0:T(128)S(1)} %fusion.44), kind=kOutput, calls=%fused_computation.14 | convolution fusion | flops 340278272 | bytes 4276480 | tf_op jit(solution)/shard_map/while/body/eval_jaxpr/nj,jcb->ncb/dot_general | solution.py:89
  122.9 49.0 %all-to-all-done = bf16[8,64,4096]{2,1,0:T(8,128)(2,1)} async-done(((bf16[8,64,4096]{2,1,0:T(8,128)(2,1)}), bf16[8,64,4096]{2,1,0:T(8,128)(2,1)}, u32[]{:S(2)}, u32[]{:S(2)}) %all-to-all-start) | async-done | bytes 4194336 | tf_op jit(solution)/shard_map/all_to_all | solution.py:150
  171.9 3.0 %convert_reduce_fusion = f32[64,4096]{1,0:T(8,128)S(1)} fusion(bf16[8,64,4096]{2,1,0:T(8,128)(2,1)} %all-to-all-done), kind=kLoop, calls=%fused_computation.4 | loop fusion | flops 3932160 | bytes 5242880 | tf_op jit(solution)/shard_map/reduce_sum | solution.py:153
  175.3 0.3 fusion.53
  175.6 6.3 %fusion.7 = bf16[64,32,128]{2,1,0:T(8,128)(2,1)S(1)} fusion(bf16[64,256,128]{2,0,1:T(8,128)(2,1)} %fusion.6, bf16[64,32,128]{2,1,0:T(8,128)(2,1)S(1)} %get-tuple-element.1201, bf16[64,32,128]{2,1,0:T(8,128)(2,1)S(1)} %get-tuple-element.1200), kind=kOutput, calls=%fused_computation.15 | convolution fusion | flops 136577024 | bytes 5767168 | tf_op jit(solution)/shard_map/while/body/eval_jaxpr/nac,ncb->nab/dot_general | solution.py:94
  182.2 0.3 fusion.2
  182.6 1.2 copy.175
  183.8 3.6 %all-to-all-start.2 = ((bf16[4,16,4096]{2,0,1:T(4,128)(2,1)}), bf16[4,16,4096]{2,0,1:T(4,128)(2,1)S(1)}, u32[]{:S(2)}, u32[]{:S(2)}) async-start(bf16[4,16,4096]{2,0,1:T(4,128)(2,1)} %copy.175), calls=%async_computation.2 | async-start | bytes 1048576 | tf_op jit(solution)/shard_map/all_to_all | solution.py:190
  187.5 6.6 %gather_fusion.1 = f32[1024]{0:T(1024)S(1)} fusion(f32[32]{0:T(128)S(1)} %copy-done, s32[1024]{0:T(1024)S(1)} %broadcast_clamp_fusion), kind=kCustom, calls=%fused_computation.1 | custom fusion | bytes 12288 | tf_op jit(solution)/shard_map/jit(_take)/gather | solution.py:33
  194.3 7.8 %all-to-all-done.2 = bf16[4,16,4096]{2,0,1:T(4,128)(2,1)S(1)} async-done(((bf16[4,16,4096]{2,0,1:T(4,128)(2,1)}), bf16[4,16,4096]{2,0,1:T(4,128)(2,1)S(1)}, u32[]{:S(2)}, u32[]{:S(2)}) %all-to-all-start.2) | async-done | bytes 524320 | tf_op jit(solution)/shard_map/all_to_all | solution.py:190
  202.4 1.2 fusion.3
  (551 shorter events, 18.8 us)
Async XLA Ops:
  0.0 187.5 %copy-start = (f32[32]{0:T(128)S(1)}, f32[32]{0:T(128)}, u32[]{:S(2)}) copy-start(f32[32]{0:T(128)} %param.173) | copy-start | bytes 388
  3.7 3.3 %copy-start.5 = (bf16[1,512,4096]{2,1,0:T(8,128)(2,1)S(1)}, bf16[1,512,4096]{2,1,0:T(8,128)(2,1)}, u32[]{:S(2)}) copy-start(bf16[1,512,4096]{2,1,0:T(8,128)(2,1)} %param.168) | copy-start | bytes 12582916
  7.0 3.2 %copy-start.6 = (s32[1,512]{1,0:T(1,128)S(1)}, s32[1,512]{1,0:T(1,128)}, u32[]{:S(2)}) copy-start(s32[1,512]{1,0:T(1,128)} %param.170) | copy-start | bytes 6148
  7.0 3.2 %copy-start.7 = (s32[1,512,1]{1,2,0:T(1,128)S(1)}, s32[1,512,1]{1,2,0:T(1,128)}, u32[]{:S(2)}) copy-start(s32[1,512,1]{1,2,0:T(1,128)} %param.169) | copy-start | bytes 6148
  10.2 2.2 %copy-start.1 = (bf16[64,8,32,128]{3,2,1,0:T(8,128)(2,1)S(1)}, bf16[64,8,32,128]{3,2,1,0:T(8,128)(2,1)}, u32[]{:S(2)}) copy-start(bf16[64,8,32,128]{3,2,1,0:T(8,128)(2,1)} %copy.182) | copy-start | bytes 12582916
  12.4 2.2 %copy-start.2 = (bf16[64,8,32,128]{3,2,1,0:T(8,128)(2,1)S(1)}, bf16[64,8,32,128]{3,2,1,0:T(8,128)(2,1)}, u32[]{:S(2)}) copy-start(bf16[64,8,32,128]{3,2,1,0:T(8,128)(2,1)} %copy.181) | copy-start | bytes 12582916
  55.7 8.8 %copy-start.3 = (f32[16]{0:T(128)S(1)}, f32[16]{0:T(128)}, u32[]{:S(2)}) copy-start(f32[16]{0:T(128)} %param.172) | copy-start | bytes 196
  57.1 16.1 %all-to-all-start.1 = ((f32[8,64,128]{2,1,0:T(8,128)}), f32[8,64,128]{2,1,0:T(8,128)S(1)}, u32[]{:S(2)}, u32[]{:S(2)}) async-start(f32[8,64,128]{2,1,0:T(8,128)} %bitcast.6), calls=%async_computation.1 | async-start | bytes 524288 | tf_op jit(solution)/shard_map/all_to_all | solution.py:155
  73.2 18.4 %copy-start.4 = (f32[80,64]{1,0:T(8,128)S(1)}, f32[80,64]{1,0:T(8,128)}, u32[]{:S(2)}) copy-start(f32[80,64]{1,0:T(8,128)} %constant.1923.clone.1) | copy-start | bytes 61444
  73.2 18.4 %copy-start.8 = (f32[2,64]{1,0:T(2,128)S(1)}, f32[2,64]{1,0:T(2,128)}, u32[]{:S(2)}) copy-start(f32[2,64]{1,0:T(2,128)} %constant.1925.clone.1) | copy-start | bytes 1540
  73.2 18.4 %copy-start.9 = (f32[2,64]{1,0:T(2,128)S(1)}, f32[2,64]{1,0:T(2,128)}, u32[]{:S(2)}) copy-start(f32[2,64]{1,0:T(2,128)} %constant.1926.clone.1) | copy-start | bytes 1540
  73.2 98.7 %all-to-all-start = ((bf16[8,64,4096]{2,1,0:T(8,128)(2,1)}), bf16[8,64,4096]{2,1,0:T(8,128)(2,1)}, u32[]{:S(2)}, u32[]{:S(2)}) async-start(bf16[8,64,4096]{2,1,0:T(8,128)(2,1)} %bitcast.309), calls=%async_computation | async-start | bytes 8388608 | tf_op jit(solution)/shard_map/all_to_all | solution.py:150
  183.8 18.3 %all-to-all-start.2 = ((bf16[4,16,4096]{2,0,1:T(4,128)(2,1)}), bf16[4,16,4096]{2,0,1:T(4,128)(2,1)S(1)}, u32[]{:S(2)}, u32[]{:S(2)}) async-start(bf16[4,16,4096]{2,0,1:T(4,128)(2,1)} %copy.175), calls=%async_computation.2 | async-start | bytes 1048576 | tf_op jit(solution)/shard_map/all_to_all | solution.py:190
